TPU v7x, 32 devices: a whole 2x2x4 slice. The times are simulated.
32 devices in a mesh: grp: 2 (over core), fsdp: 8 (over z, x), tp: 2 (over y).
Axes of the slice: x: 2, y: 2, z: 4, core: 2. Of those that a mesh axis runs over, the one named last changes fastest.
Arguments:
- normed_inputs: bfloat16 [12288, 8192], P(('grp', 'fsdp')), may hold values from -6 to 6
- value_cotangent: bfloat16 [12288, 1024], P(('grp', 'fsdp'), 'tp'), may hold values from -0.0546875 to 0.0546875
- value_weight: bfloat16 [8192, 1024], P(('grp', 'fsdp'), 'tp'), may hold values from -0.0625 to 0.0625
- decode_inputs: bfloat16 [256, 4, 8192], P(('grp', 'fsdp'), None, 'tp'), may hold values from -6 to 6
- queries: bfloat16 [256, 4, 8192], P(('grp', 'fsdp'), None, 'tp')
- new_keys: bfloat16 [256, 4, 1024], P(('grp', 'fsdp'), None, 'tp'), may hold values from -6 to 6
- cache_keys: bfloat16 [256, 128, 1024], P(('grp', 'fsdp'), None, 'tp')
- cache_values: bfloat16 [256, 128, 1024], P(('grp', 'fsdp'), None, 'tp'), may hold values from -6 to 6
- lengths: int32 [256], P(('grp', 'fsdp')), may hold values from 2 to 128, as said below
Outputs:
- gradient: float32 [8192, 1024], P(('grp', 'fsdp'), 'tp')
- new_values: bfloat16 [256, 4, 1024], P(('grp', 'fsdp'), None, 'tp')
- attended: bfloat16 [256, 4, 8192], P(('grp', 'fsdp'), None, 'tp')
Inputs may be any that keep to these rules, and one draw needn't show every extreme that they name: `lengths`: at least 2 and at most 128; some row has exactly 128.
All inputs are finite; a program needn't handle non-finite values.
Results may differ from a plain program's by a relative error of at most 0.0052.
Values may be sent and summed in bfloat16 or wider, within the bound.
A program may use at most 64 MiB of HBM per device.

v0:
```python
import math

import jax
import jax.numpy as jnp
from jax import lax
from jax.sharding import PartitionSpec as P

D = 8192
QH = 64
KVH = 8
HD = 128


def attend_rows(queries, new_keys, new_values, cache_keys, cache_values, lengths):
    row_count = queries.shape[0]
    step_count = queries.shape[1]
    slot_count = cache_keys.shape[1]
    group_count = cache_keys.shape[2] // HD
    per_group = QH // KVH
    factor = 1.0 / math.sqrt(HD)
    query_heads = queries.reshape(row_count, step_count, group_count, per_group, HD)
    cached_keys = cache_keys.reshape(row_count, slot_count, group_count, HD)
    cached_values = cache_values.reshape(row_count, slot_count, group_count, HD)
    fresh_keys = new_keys.reshape(row_count, step_count, group_count, HD)
    fresh_values = new_values.reshape(row_count, step_count, group_count, HD)
    cache_scores = (
        jnp.einsum(
            "rsgqd,rpgd->rsgqp", query_heads, cached_keys, preferred_element_type=jnp.float32
        )
        * factor
    )
    live_slots = jnp.arange(slot_count, dtype=jnp.int32)[None, :] < lengths[:, None]
    cache_scores = jnp.where(live_slots[:, None, None, None, :], cache_scores, -1e30)
    fresh_scores = (
        jnp.einsum("rsgqd,rugd->rsgqu", query_heads, fresh_keys, preferred_element_type=jnp.float32)
        * factor
    )
    causal = (
        jnp.arange(step_count, dtype=jnp.int32)[None, :]
        <= jnp.arange(step_count, dtype=jnp.int32)[:, None]
    )
    fresh_scores = jnp.where(causal[None, :, None, None, :], fresh_scores, -1e30)
    highest = jnp.maximum(jnp.max(cache_scores, axis=-1), jnp.max(fresh_scores, axis=-1))
    cache_exp = jnp.exp(cache_scores - highest[..., None])
    fresh_exp = jnp.exp(fresh_scores - highest[..., None])
    denominator = jnp.sum(cache_exp, axis=-1) + jnp.sum(fresh_exp, axis=-1)
    cache_weights = (cache_exp / denominator[..., None]).astype(jnp.bfloat16)
    fresh_weights = (fresh_exp / denominator[..., None]).astype(jnp.bfloat16)
    mixed = jnp.einsum(
        "rsgqp,rpgd->rsgqd", cache_weights, cached_values, preferred_element_type=jnp.float32
    )
    mixed = mixed + jnp.einsum(
        "rsgqu,rugd->rsgqd", fresh_weights, fresh_values, preferred_element_type=jnp.float32
    )
    return mixed.astype(jnp.bfloat16).reshape(row_count, step_count, group_count * per_group * HD)


def shards(
    normed_inputs,
    value_cotangent,
    value_weight,
    decode_inputs,
    queries,
    new_keys,
    cache_keys,
    cache_values,
    lengths,
):
    step_size = 0.4 / math.sqrt(D)
    gradient = lax.psum_scatter(
        lax.dot_general(
            normed_inputs,
            value_cotangent,
            (((0,), (0,)), ((), ())),
            preferred_element_type=jnp.float32,
        ),
        ("grp", "fsdp"),
        scatter_dimension=0,
        tiled=True,
    )
    updated_shard = (value_weight.astype(jnp.float32) - step_size * gradient).astype(jnp.bfloat16)
    updated = lax.all_gather(updated_shard, ("grp", "fsdp"), axis=0, tiled=True)
    features_all = lax.all_gather(decode_inputs, "tp", axis=2, tiled=True)
    row_count = features_all.shape[0]
    step_count = features_all.shape[1]
    flat_inputs = features_all.reshape(row_count * step_count, D)
    new_values = jnp.dot(flat_inputs, updated, preferred_element_type=jnp.float32).astype(
        jnp.bfloat16
    )
    new_values = new_values.reshape(row_count, step_count, updated.shape[1])
    attended = attend_rows(queries, new_keys, new_values, cache_keys, cache_values, lengths)
    return (gradient, new_values, attended)


def solution(mesh):
    return jax.shard_map(
        shards,
        mesh=mesh,
        in_specs=(
            P(("grp", "fsdp"), None),
            P(("grp", "fsdp"), "tp"),
            P(("grp", "fsdp"), "tp"),
            P(("grp", "fsdp"), None, "tp"),
            P(("grp", "fsdp"), None, "tp"),
            P(("grp", "fsdp"), None, "tp"),
            P(("grp", "fsdp"), None, "tp"),
            P(("grp", "fsdp"), None, "tp"),
            P(("grp", "fsdp")),
        ),
        out_specs=(
            P(("grp", "fsdp"), "tp"),
            P(("grp", "fsdp"), None, "tp"),
            P(("grp", "fsdp"), None, "tp"),
        ),
        check_vma=False,
    )
```

profile of v0, /device:TPU:0, one launch (start us, length us, event | category | flops | bytes accessed | tf_op | source)
XLA Modules:
  0.0 297.1 jit_solution(10954471362287401695)
XLA Ops:
  8.0 0.0 copy-start
  8.0 0.0 reduce-scatter.2.cloned.1.call-start
  8.1 1.1 copy-done
  9.1 14.9 %fusion.33 = f32[8192,512]{1,0:T(8,128)} fusion(bf16[768,8192]{1,0:T(8,128)(2,1)} %param.9, bf16[768,512]{1,0:T(8,128)(2,1)S(1)} %copy-done), kind=kOutput, calls=%fused_computation.35 | convolution fusion | flops 6442450944 | bytes 30146560 | tf_op jit(solution)/shard_map/dot_general | solution.py:71
  24.1 0.0 reduce-scatter.2.cloned.1.call-update
  24.1 0.0 copy-start.1
  24.1 0.0 all-gather.5.cloned.1.call-start
  24.2 0.5 all-gather.5.cloned.1.call-update
  24.7 0.0 all-gather.3.cloned.1.call-start
  24.7 180.7 %reduce-scatter.2.cloned.1.call-done = f32[512,512]{1,0:T(8,128)} async-done(((f32[8192,512]{1,0:T(8,128)}), f32[512,512]{1,0:T(8,128)}) %reduce-scatter.2.cloned.1.call-update) | async-done | bytes 1048592 | tf_op jit(solution)/shard_map/reduce_scatter | solution.py:70
  205.5 2.2 subtract_convert_fusion
  207.7 0.0 all-gather.3.cloned.1.call-update
  207.7 0.0 copy-done.1
  207.7 0.0 copy-start.3
  207.7 2.1 reshape.71
  209.8 1.4 reshape.69
  211.2 2.6 reshape.68
  213.8 0.0 copy-done.5
  213.8 0.1 iota_compare_fusion
  213.9 3.5 %fusion.32 = (f32[16,4,4,8]{3,1,2,0:T(4,128)S(1)}, f32[16,4,4,8,4]{3,4,1,2,0:T(4,128)S(1)}) fusion(bf16[16,4,4,8,128]{4,3,2,1,0:T(8,128)(2,1)} %reshape.69, bf16[16,4,512]{2,1,0:T(4,128)(2,1)S(1)} %copy-done.6, pred[4,4]{1,0:T(4,128)(4,1)S(1)} %iota_compare_fusion.1), kind=kOutput, calls=%fused_computation.34 | convolution fusion | flops 2119680 | bytes 630800 | tf_op jit(solution)/shard_map/rsgqd,rugd->rsgqu/dot_general | solution.py:35
  217.4 2.4 fusion.31
  219.8 0.5 fusion.26
  220.3 0.8 fusion.21
  221.1 0.2 copy-done.2
  221.4 1.8 fusion.4
  223.2 1.3 reshape.66
  224.5 56.8 %all-gather.3.cloned.1.call-done = bf16[8192,512]{1,0:T(8,128)(2,1)} async-done(((bf16[512,512]{1,0:T(8,128)(2,1)}), bf16[8192,512]{1,0:T(8,128)(2,1)}) %all-gather.3.cloned.1.call-update) | async-done | bytes 8388624 | tf_op jit(solution)/shard_map/all_gather | solution.py:82
  281.3 4.9 %fusion.20 = bf16[64,512]{1,0:T(8,128)(2,1)S(1)} fusion(bf16[64,8192]{1,0:T(8,128)(2,1)S(1)} %reshape.66, bf16[8192,512]{1,0:T(8,128)(2,1)} %all-gather.3.cloned.1.call-done), kind=kOutput, calls=%fused_computation.15 | convolution fusion | flops 536903680 | bytes 9502720 | tf_op jit(solution)/shard_map/dot_general | solution.py:87
  286.2 0.7 reshape.67
  286.9 1.7 fusion.17
  288.6 0.1 copy.36
  288.7 0.9 reshape.77
  (12 shorter events, 0.1 us)
Async XLA Ops:
  8.0 1.1 copy-start
  8.0 197.5 %reduce-scatter.2.cloned.1.call-start = ((), (), s32[]{:S(2)}) async-start(), calls=%async_computation.1 | async-start | bytes 17825792 | tf_op jit(solution)/shard_map/reduce_scatter | solution.py:70
  24.1 181.4 %copy-start.4 = (bf16[512,512]{1,0:T(8,128)(2,1)S(1)}, bf16[512,512]{1,0:T(8,128)(2,1)}, u32[]{:S(2)}) copy-start(bf16[512,512]{1,0:T(8,128)(2,1)} %param.11) | copy-start | bytes 1572868
  24.1 183.6 %copy-start.1 = (bf16[16,128,512]{2,1,0:T(8,128)(2,1)S(1)}, bf16[16,128,512]{2,1,0:T(8,128)(2,1)}, u32[]{:S(2)}) copy-start(bf16[16,128,512]{2,1,0:T(8,128)(2,1)} %param.16) | copy-start | bytes 6291460
  24.1 199.1 %all-gather.5.cloned.1.call-start = ((), (), s32[]{:S(2)}) async-start(), calls=%async_computation.3 | async-start | bytes 1572864 | tf_op jit(solution)/shard_map/all_gather | solution.py:83
  24.7 256.6 %all-gather.3.cloned.1.call-start = ((), (), s32[]{:S(2)}) async-start(), calls=%async_computation.2 | async-start | bytes 8912896 | tf_op jit(solution)/shard_map/all_gather | solution.py:82
  207.7 2.1 copy-start.3
  211.2 2.6 copy-start.5
  211.2 2.7 copy-start.6
  219.8 1.6 copy-start.2
Sparse Core Ops, SparseCore 0:
  24.2 181.2 reduce-scatter.1
Sparse Core Ops, SparseCore 1:
  26.1 23.8 all-gather.4
  207.8 73.4 all-gather.2
where the time goes:
time: 298 us; the launch traced here: 297 us
  waiting for transfers between devices  238 us (80%)
  matrix products  29.3 us (10%)
  between operations  15.6 us (5%)
  local copies, waits for them, and re-layouts  10.4 us (3%)
  other arithmetic  3.61 us (1%)
    reduce_scatter x1, waiting for transfers between devices, shards(): lax.psum_scatter(lax.dot_general(normed_inputs, value_cotangent, (((0,),...  181 us
    all_gather x1, waiting for transfers between devices, shards(): updated = lax.all_gather(updated_shard, ('grp', 'fsdp'), axis=0, tiled=True)  56.8 us
    dot_general x1, matrix products, shards(): lax.dot_general(normed_inputs, value_cotangent, (((0,), (0,)), ((), ())),...  14.9 us
  transfers between devices with their start and end apart: 3, of which 2 were waited for; matrix products, arithmetic and copies ran while one was open for 6% of the time, Pallas kernels for 0%

commit v1 on v0

v1 whole, which is shorter than its diff:
```python
import functools
import math

import jax
import jax.numpy as jnp
from jax import lax
from jax.experimental import pallas as pl
from jax.experimental.pallas import tpu as pltpu
from jax.sharding import PartitionSpec as P

D = 8192
QH = 64
KVH = 8
HD = 128
LANES = 256
CHUNK = 128
MESH = pl.DeviceIdType.MESH
BF16 = jnp.bfloat16
F32 = jnp.float32


def attend_rows(queries, new_keys, new_values, cache_keys, cache_values, lengths):
    row_count = queries.shape[0]
    step_count = queries.shape[1]
    slot_count = cache_keys.shape[1]
    group_count = cache_keys.shape[2] // HD
    per_group = QH // KVH
    factor = 1.0 / math.sqrt(HD)
    query_heads = queries.reshape(row_count, step_count, group_count, per_group, HD)
    cached_keys = cache_keys.reshape(row_count, slot_count, group_count, HD)
    cached_values = cache_values.reshape(row_count, slot_count, group_count, HD)
    fresh_keys = new_keys.reshape(row_count, step_count, group_count, HD)
    fresh_values = new_values.reshape(row_count, step_count, group_count, HD)
    cache_scores = (
        jnp.einsum("rsgqd,rpgd->rsgqp", query_heads, cached_keys, preferred_element_type=F32)
        * factor
    )
    live_slots = jnp.arange(slot_count, dtype=jnp.int32)[None, :] < lengths[:, None]
    cache_scores = jnp.where(live_slots[:, None, None, None, :], cache_scores, -1e30)
    fresh_scores = (
        jnp.einsum("rsgqd,rugd->rsgqu", query_heads, fresh_keys, preferred_element_type=F32)
        * factor
    )
    causal = (
        jnp.arange(step_count, dtype=jnp.int32)[None, :]
        <= jnp.arange(step_count, dtype=jnp.int32)[:, None]
    )
    fresh_scores = jnp.where(causal[None, :, None, None, :], fresh_scores, -1e30)
    highest = jnp.maximum(jnp.max(cache_scores, axis=-1), jnp.max(fresh_scores, axis=-1))
    cache_exp = jnp.exp(cache_scores - highest[..., None])
    fresh_exp = jnp.exp(fresh_scores - highest[..., None])
    denominator = jnp.sum(cache_exp, axis=-1) + jnp.sum(fresh_exp, axis=-1)
    cache_weights = (cache_exp / denominator[..., None]).astype(BF16)
    fresh_weights = (fresh_exp / denominator[..., None]).astype(BF16)
    mixed = jnp.einsum(
        "rsgqp,rpgd->rsgqd", cache_weights, cached_values, preferred_element_type=F32
    )
    mixed = mixed + jnp.einsum(
        "rsgqu,rugd->rsgqd", fresh_weights, fresh_values, preferred_element_type=F32
    )
    return mixed.astype(BF16).reshape(row_count, step_count, group_count * per_group * HD)


def kernel(
    F, T, stages, x_hbm, dyt, w, dec, grad, nv,
    xbuf, acc, a_send, a_recv, decpos, u, nva, *rest
):
    n = 2 * F
    k_s = rest[: stages - 1]
    k_r = rest[stages - 1 : 2 * stages - 2]
    n_s = rest[2 * stages - 2 : 3 * stages - 2]
    n_r = rest[3 * stages - 2 : 4 * stages - 2]
    (x_sem, a_ssem, a_rsem, k_ssem, k_rsem, n_ssem, n_rsem, d_ssem, d_rsem, f_ssem, f_rsem,
     own_sem) = rest[4 * stages - 2 :]
    cols = dyt.shape[0]
    block = w.shape[0]
    halves = block // LANES
    parts = cols // CHUNK
    tokens = dec.shape[0]
    quarter = n // 4
    step_size = 0.4 / math.sqrt(D)
    g = lax.axis_index("grp")
    f = lax.axis_index("fsdp")
    t = lax.axis_index("tp")

    def place(p):
        g2 = 1 - g if (p >> (stages - 1)) & 1 else g
        f2 = f
        for bit in range(stages - 1):
            if (p >> (stages - 2 - bit)) & 1:
                f2 = f2 + (1 - 2 * ((f // (1 << bit)) % 2)) * (1 << bit)
        return g2, f2

    def partner(stage):
        return place(n >> (stage + 1)) + (t,)

    def x_copy(h, p):
        g2, f2 = place(p)
        start = pl.multiple_of((g2 * F + f2) * block + h * LANES, LANES)
        slot = h * n + p
        return pltpu.make_async_copy(
            x_hbm.at[:, pl.ds(start, LANES)], xbuf.at[slot], x_sem.at[slot]
        )

    order = [(h, q) for h in range(halves) for q in (3, 1)]
    order += [(h, q) for h in range(halves) for q in (2, 0)]
    for h, q in order:
        for p in range(q * quarter, (q + 1) * quarter):
            x_copy(h, p).start()

    barrier = pltpu.get_barrier_semaphore()
    for p in range(1, n):
        g2, f2 = place(p)
        pl.semaphore_signal(barrier, inc=1, device_id=(g2, f2, t), device_id_type=MESH)
    for d in range(1, T):
        pl.semaphore_signal(
            barrier, inc=1, device_id=(g, f, lax.rem(t + d, T)), device_id_type=MESH
        )
    pl.semaphore_wait(barrier, n - 1 + T - 1)

    share = n // T
    me = g * F + f
    is_root = me // share == t

    def dec_copy(p):
        g2, f2 = place(p)
        owner = g2 * F + f2
        start = pl.multiple_of((owner % share) * block, block)
        return owner // share == t, pltpu.make_async_remote_copy(
            src_ref=dec.at[:, pl.ds(start, block)],
            dst_ref=decpos.at[p],
            send_sem=d_ssem.at[p],
            recv_sem=d_rsem.at[p],
            device_id=(g2, f2, t),
            device_id_type=MESH,
        )

    own_start = pl.multiple_of((me % share) * block, block)
    own_copy = pltpu.make_async_copy(dec.at[:, pl.ds(own_start, block)], decpos.at[0], own_sem)

    @pl.when(is_root)
    def _():
        own_copy.start()

    for p in range(1, n):
        wanted, copy = dec_copy(p)
        pl.when(wanted)(copy.start)

    def forward(d):
        return pltpu.make_async_remote_copy(
            src_ref=decpos,
            dst_ref=decpos,
            send_sem=f_ssem.at[d],
            recv_sem=f_rsem,
            device_id=(g, f, lax.rem(t + d, T)),
            device_id_type=MESH,
        )

    def pass_on():
        @pl.when(is_root)
        def _():
            own_copy.wait()
            for p in range(1, n):
                dec_copy(p)[1].wait_recv()
            for d in range(1, T):
                forward(d).start()

    def multiply(h, q, store):
        for p in range(q * quarter, (q + 1) * quarter):
            x_copy(h, p).wait()

        def body(i, _):
            store(
                i,
                jnp.dot(dyt[...], xbuf[h * n + q * quarter + i], preferred_element_type=F32),
            )
            return 0

        lax.fori_loop(0, quarter, body, 0)

    def a_copy(h, q):
        return pltpu.make_async_remote_copy(
            src_ref=a_send.at[h, q],
            dst_ref=a_recv.at[h, q],
            send_sem=a_ssem.at[h, q],
            recv_sem=a_rsem.at[h, q],
            device_id=partner(0),
            device_id_type=MESH,
        )

    def for_partner(h, q):
        def store(i, value):
            a_send[h, q, i] = value.astype(BF16)

        multiply(h, q + 2, store)
        a_copy(h, q).start()

    def for_self(h, q):
        def store(i, value):
            acc[h, q * quarter + i] = value

        multiply(h, q, store)

    def k_copy(stage, c, h):
        k = c * halves + h
        return pltpu.make_async_remote_copy(
            src_ref=k_s[stage - 1].at[k],
            dst_ref=k_r[stage - 1].at[k],
            send_sem=k_ssem.at[stage - 1, k],
            recv_sem=k_rsem.at[stage - 1, k],
            device_id=partner(stage),
            device_id_type=MESH,
        )

    def first_send(c, h):
        cs = pl.ds(c * CHUNK, CHUNK)
        for i in range(quarter):
            k_s[0][c * halves + h, i] = (
                acc[h, quarter + i, cs, :] + a_recv[h, 1, i, cs, :].astype(F32)
            ).astype(BF16)
        k_copy(1, c, h).start()

    def reduce(stage, c, h):
        cs = pl.ds(c * CHUNK, CHUNK)
        k = c * halves + h
        count = n >> (stage + 1)
        k_copy(stage, c, h).wait_recv()
        if stage == 1 and c == 0:
            a_copy(h, 0).wait_recv()
        last = stage == stages - 1
        for i in range(count - 1, -1, -1):
            value = acc[h, i, cs, :] + k_r[stage - 1][k, i].astype(F32)
            if stage == 1:
                value = value + a_recv[h, 0, i, cs, :].astype(F32)
            if last:
                value = value.T
                hs = pl.ds(h * LANES, LANES)
                grad[hs, cs] = value
                u[hs, cs] = (w[hs, cs].astype(F32) - step_size * value).astype(BF16)
            elif i >= count // 2:
                k_s[stage][k, i - count // 2] = value.astype(BF16)
            else:
                acc[h, i, cs, :] = value
            if not last and i == count // 2:
                k_copy(stage + 1, c, h).start()

    def n_copy(stage, c):
        return pltpu.make_async_remote_copy(
            src_ref=n_s[stage].at[c],
            dst_ref=n_r[stage].at[c],
            send_sem=n_ssem.at[stage, c],
            recv_sem=n_rsem.at[stage, c],
            device_id=partner(stage),
            device_id_type=MESH,
        )

    def project(c):
        if c == 0:

            @pl.when(jnp.logical_not(is_root))
            def _():
                forward(1).wait_recv()

        cs = pl.ds(c * CHUNK, CHUNK)
        weight = u[:, cs]
        half = n // 2
        high = decpos[half:].reshape(half * tokens, block)
        n_s[0][c] = (
            jnp.dot(high, weight, preferred_element_type=F32)
            .astype(BF16)
            .reshape(half, tokens, CHUNK)
        )
        n_copy(0, c).start()
        low = decpos[:half].reshape(half * tokens, block)
        nva[c] = jnp.dot(low, weight, preferred_element_type=F32).reshape(half, tokens, CHUNK)

    def n_reduce(stage, c):
        count = n >> (stage + 1)
        n_copy(stage, c).wait_recv()
        value = nva[c, :count] + n_r[stage][c].astype(F32)
        if stage == stages - 1:
            nv[:, c * CHUNK : (c + 1) * CHUNK] = value[0].astype(BF16)
        else:
            n_s[stage + 1][c] = value[count // 2 :].astype(BF16)
            n_copy(stage + 1, c).start()
            nva[c, : count // 2] = value[: count // 2]

    chunks = [(c, h) for c in range(parts) for h in range(halves)]

    for_partner(0, 1)
    for_self(0, 1)
    for h in range(1, halves):
        for_partner(h, 1)
    a_copy(0, 1).wait_recv()
    first_send(0, 0)
    for h in range(1, halves):
        for_self(h, 1)
        a_copy(h, 1).wait_recv()
    for c, h in chunks[1:]:
        first_send(c, h)
    for h in range(halves):
        for_partner(h, 0)
    for h in range(halves):
        for_self(h, 0)
    pass_on()

    pending = []

    def slot():
        if pending:
            what, stage, c = pending.pop(0)
            if what == 0:
                project(c)
            else:
                n_reduce(stage, c)

    def finish(j):
        c, h = chunks[j]
        if h == halves - 1:
            pending.append((0, 0, c))
            pending.extend((1, s, c) for s in range(stages))

    def stage_of(stage, j):
        if 0 <= j < len(chunks):
            reduce(stage, *chunks[j])
            if stage == stages - 1:
                finish(j)

    for j in range(len(chunks) + stages):
        stage_of(1, j)
        for stage in range(3, stages):
            stage_of(stage, j - (stage - 2))
        slot()
        if j < len(chunks) - 1:
            slot()
        stage_of(2, j)
        slot()
    while pending:
        slot()

    for h in range(halves):
        for q in (0, 1):
            a_copy(h, q).wait_send()
    for c, h in chunks:
        for stage in range(1, stages):
            k_copy(stage, c, h).wait_send()
    for c in range(parts):
        for stage in range(stages):
            n_copy(stage, c).wait_send()
    for p in range(1, n):
        wanted, copy = dec_copy(p)
        pl.when(wanted)(copy.wait_send)

    @pl.when(is_root)
    def _():
        for d in range(1, T):
            forward(d).wait_send()


def exchange(F, T, x, dyt, w, dec):
    n = 2 * F
    stages = n.bit_length() - 1
    cols = dyt.shape[0]
    held = x.shape[0]
    block = w.shape[0]
    halves = block // LANES
    parts = cols // CHUNK
    tokens = dec.shape[0]
    count = halves * parts
    dma = pltpu.SemaphoreType.DMA
    k_bufs = [
        pltpu.VMEM((count, n >> (s + 1), CHUNK, LANES), BF16) for s in range(1, stages)
    ]
    n_bufs = [pltpu.VMEM((parts, n >> (s + 1), tokens, CHUNK), BF16) for s in range(stages)]
    vmem = pl.BlockSpec(memory_space=pltpu.VMEM)
    hbm = pl.BlockSpec(memory_space=pl.ANY)
    return pl.pallas_call(
        functools.partial(kernel, F, T, stages),
        out_shape=(
            jax.ShapeDtypeStruct((block, cols), F32),
            jax.ShapeDtypeStruct((tokens, cols), BF16),
        ),
        in_specs=[hbm, vmem, vmem, hbm],
        out_specs=(vmem, vmem),
        scratch_shapes=[
            pltpu.VMEM((halves * n, held, LANES), BF16),
            pltpu.VMEM((halves, n // 2, cols, LANES), F32),
            pltpu.VMEM((halves, 2, n // 4, cols, LANES), BF16),
            pltpu.VMEM((halves, 2, n // 4, cols, LANES), BF16),
            pltpu.VMEM((n, tokens, block), BF16),
            pltpu.VMEM((block, cols), BF16),
            pltpu.VMEM((parts, n // 2, tokens, CHUNK), F32),
            *k_bufs,
            *k_bufs,
            *n_bufs,
            *n_bufs,
            dma((halves * n,)),
            dma((halves, 2)),
            dma((halves, 2)),
            dma((stages - 1, count)),
            dma((stages - 1, count)),
            dma((stages, parts)),
            dma((stages, parts)),
            dma((n,)),
            dma((n,)),
            dma((T,)),
            dma,
            dma,
        ],
        compiler_params=pltpu.CompilerParams(
            collective_id=0, has_side_effects=True, vmem_limit_bytes=58 * 2**20
        ),
        cost_estimate=pl.CostEstimate(
            flops=2 * held * D * cols, bytes_accessed=held * D * 2, transcendentals=0
        ),
    )(x, dyt, w, dec)


def shards(
    F,
    T,
    normed_inputs,
    value_cotangent,
    value_weight,
    decode_inputs,
    queries,
    new_keys,
    cache_keys,
    cache_values,
    lengths,
):
    rows, steps, features = decode_inputs.shape
    gradient, flat_values = exchange(
        F,
        T,
        normed_inputs,
        value_cotangent.T,
        value_weight,
        decode_inputs.reshape(rows * steps, features),
    )
    new_values = flat_values.reshape(rows, steps, flat_values.shape[1])
    attended = attend_rows(queries, new_keys, new_values, cache_keys, cache_values, lengths)
    return (gradient, new_values, attended)


def solution(mesh):
    return jax.shard_map(
        functools.partial(shards, mesh.shape["fsdp"], mesh.shape["tp"]),
        mesh=mesh,
        in_specs=(
            P(("grp", "fsdp"), None),
            P(("grp", "fsdp"), "tp"),
            P(("grp", "fsdp"), "tp"),
            P(("grp", "fsdp"), None, "tp"),
            P(("grp", "fsdp"), None, "tp"),
            P(("grp", "fsdp"), None, "tp"),
            P(("grp", "fsdp"), None, "tp"),
            P(("grp", "fsdp"), None, "tp"),
            P(("grp", "fsdp")),
        ),
        out_specs=(
            P(("grp", "fsdp"), "tp"),
            P(("grp", "fsdp"), None, "tp"),
            P(("grp", "fsdp"), None, "tp"),
        ),
        check_vma=False,
    )
```

time: 298 us -> 142 us (0.48)
  waiting for transfers between devices: 238 us -> 0 us
  Pallas kernels: 0 us -> 119 us
  matrix products: 29.3 us -> 8.75 us
  between operations: 15.6 us -> 0.79 us
    reduce_scatter x1 -> x0, waiting for transfers between devices: 181 us -> none  [shards(): lax.psum_scatter(lax.dot_general(normed_inputs, value_cotangent, (((0,),...]
    pallas_call x0 -> x1, Pallas kernels: none -> 119 us  [exchange(): pl.pallas_call(functools.partial(kernel, F, T, stages), out_shape=(jax.Sh...]
    all_gather x2 -> x0, waiting for transfers between devices: 56.8 us -> none  [the longest x1 56.8 us: shards(): updated = lax.all_gather(updated_shard, ('grp', 'fsdp'), axis=0, tiled=True)]
    dot_general x2 -> x0, matrix products: 19.9 us -> none  [the longest x1 14.9 us: shards(): lax.dot_general(normed_inputs, value_cotangent, (((0,), (0,)), ((), ())),...]
  transfers between devices with their start and end apart: 3 -> 0, of which waited for: 2 -> 0; matrix products, arithmetic and copies ran while one was open for 6% -> 0% of each run, Pallas kernels for 0% -> 0%
where the time goes in v1:
time: 142 us
  Pallas kernels  119 us (84%)
  local copies, waits for them, and re-layouts  12.7 us (9%)
  matrix products  8.75 us (6%)
  other arithmetic  1.42 us (1%)
    pallas_call x1, Pallas kernels, exchange(): pl.pallas_call(functools.partial(kernel, F, T, stages), out_shape=(jax.Sh...  119 us
    dot_general x1, matrix products, attend_rows(): jnp.einsum('rsgqp,rpgd->rsgqd', cache_weights, cached_values, preferred_e...  3.39 us
    unnamed x26, local copies, waits for them, and re-layouts  3.22 us

profile of v1, /device:TPU:0, one launch (start us, length us, event | category | flops | bytes accessed | tf_op | source)
XLA Modules:
  0.0 142.2 jit_solution(1309671625575600555)
XLA Ops:
  0.6 0.0 copy-start
  0.6 2.4 %reshape.69 = bf16[16,4,4,8,128]{4,3,2,1,0:T(8,128)(2,1)} reshape(bf16[16,4,4096]{2,1,0:T(4,128)(2,1)} %param.13) | data formatting | bytes 1048576 | tf_op jit(solution)/shard_map/reshape | solution.py:29
  3.1 2.6 %reshape.68 = bf16[16,128,4,128]{3,2,1,0:T(4,128)(2,1)S(1)} reshape(bf16[16,128,512]{2,1,0:T(8,128)(2,1)} %param.15) | data formatting | bytes 4194304 | tf_op jit(solution)/shard_map/reshape | solution.py:30
  5.6 0.0 copy-done.9
  5.6 0.1 iota_compare_fusion
  5.7 2.4 %fusion.30 = (f32[16,4,4,8]{3,1,2,0:T(4,128)S(1)}, f32[16,4,4,8,128]{4,3,1,2,0:T(8,128)S(1)}) fusion(bf16[16,4,4,8,128]{4,3,2,1,0:T(8,128)(2,1)} %reshape.69, bf16[16,128,4,128,1]{3,2,1,0,4:T(4,128)(2,1)S(1)} %bitcast.29, pred[16,128]{1,0:T(8,128)(4,1)S(1)} %iota_compare_fusion), kind=kOutput, calls=%fused_computation.30 | convolution fusion | flops 67893248 | bytes 3680256 | tf_op jit(solution)/shard_map/rsgqd,rpgd->rsgqp/dot_general | solution.py:35
  8.1 0.0 copy-done
  8.2 0.0 copy-done.7
  8.2 0.0 copy-start.1
  8.2 2.5 %fusion.31 = (f32[16,4,4,8]{3,1,2,0:T(4,128)S(1)}, f32[16,4,4,8,4]{3,4,1,2,0:T(4,128)S(1)}) fusion(bf16[16,4,4,8,128]{4,3,2,1,0:T(8,128)(2,1)S(1)} %copy-done.7, bf16[16,4,512]{2,1,0:T(4,128)(2,1)S(1)} %copy-done, pred[4,4]{1,0:T(4,128)(4,1)S(1)} %iota_compare_fusion.1), kind=kOutput, calls=%fused_computation.31 | convolution fusion | flops 2119680 | bytes 630800 | tf_op jit(solution)/shard_map/rsgqd,rugd->rsgqu/dot_general | solution.py:41
  10.6 0.0 copy-start.4
  10.6 0.1 max.7
  10.7 0.8 fusion.20
  11.5 0.0 copy-done.4
  11.5 0.5 fusion.25
  12.0 0.0 copy-done.1
  12.0 2.1 %reshape.71 = bf16[16,128,4,128]{3,2,1,0:T(4,128)(2,1)} reshape(bf16[16,128,512]{2,1,0:T(8,128)(2,1)S(1)} %copy-done.1) | data formatting | bytes 4194304 | tf_op jit(solution)/shard_map/reshape | solution.py:31
  14.1 3.4 %fusion.4 = f32[16,4,4,8,128]{4,3,1,2,0:T(8,128)} fusion(bf16[16,128,4,128,1]{3,2,1,0,4:T(4,128)(2,1)} %bitcast.30, f32[16,4,4,8,128]{4,3,1,2,0:T(8,128)S(1)} %get-tuple-element.11, f32[16,4,4,8]{3,1,2,0:T(4,128)S(1)} %add.10, f32[16,4,4,8]{3,1,2,0:T(4,128)S(1)} %max.7), kind=kOutput, calls=%fused_computation.4 | convolution fusion | flops 67895296 | bytes 4210688 | tf_op jit(solution)/shard_map/rsgqp,rpgd->rsgqd/dot_general | solution.py:55
  17.5 0.0 copy-done.3
  17.5 1.2 copy.19
  18.7 0.0 copy-done.6
  18.7 0.9 reshape.66.dec
  19.6 118.6 %shard_map.112 = (f32[512,512]{1,0:T(8,128)}, bf16[64,512]{1,0:T(8,128)(2,1)}) custom-call(bf16[768,8192]{1,0:T(8,128)(2,1)} %x_hbm.1, bf16[512,768]{1,0:T(8,128)(2,1)} %bitcast.31, bf16[512,512]{1,0:T(8,128)(2,1)} %w.1, bf16[64,4096]{1,0:T(8,128)(2,1)} %reshape.66.dec), custom_call_target="tpu_custom_call" | custom-call | flops 6442450944 | bytes 12582912 | tf_op jit(solution)/shard_map/pallas_call | solution.py:377
  138.2 0.9 reshape_reshape.3
  139.0 0.0 copy-done.5
  139.0 0.0 copy-done.10
  139.1 0.5 fusion.17
  139.6 0.1 copy.38
  139.7 0.9 reshape.77
  140.6 0.0 copy-done.8
  140.6 0.6 reshape.67
  141.2 1.0 copy.65
  (11 shorter events, 0.1 us)
Async XLA Ops:
  0.6 7.5 %copy-start = (bf16[16,4,512]{2,1,0:T(4,128)(2,1)S(1)}, bf16[16,4,512]{2,1,0:T(4,128)(2,1)}, u32[]{:S(2)}) copy-start(bf16[16,4,512]{2,1,0:T(4,128)(2,1)} %param.14) | copy-start | bytes 196612
  3.1 2.6 %copy-start.9 = (s32[16]{0:T(128)S(1)}, s32[16]{0:T(128)}, u32[]{:S(2)}) copy-start(s32[16]{0:T(128)} %param.17) | copy-start | bytes 196
  5.7 2.4 %copy-start.7 = (bf16[16,4,4,8,128]{4,3,2,1,0:T(8,128)(2,1)S(1)}, bf16[16,4,4,8,128]{4,3,2,1,0:T(8,128)(2,1)}, u32[]{:S(2)}) copy-start(bf16[16,4,4,8,128]{4,3,2,1,0:T(8,128)(2,1)} %reshape.69) | copy-start | bytes 1572868
  8.2 3.8 %copy-start.1 = (bf16[16,128,512]{2,1,0:T(8,128)(2,1)S(1)}, bf16[16,128,512]{2,1,0:T(8,128)(2,1)}, u32[]{:S(2)}) copy-start(bf16[16,128,512]{2,1,0:T(8,128)(2,1)} %param.16) | copy-start | bytes 6291460
  10.6 0.8 copy-start.4
  14.1 3.4 %copy-start.3 = (bf16[768,512]{1,0:T(8,128)(2,1)S(1)}, bf16[768,512]{1,0:T(8,128)(2,1)}, u32[]{:S(2)}) copy-start(bf16[768,512]{1,0:T(8,128)(2,1)} %param.10) | copy-start | bytes 2359300
  14.1 4.6 %copy-start.6 = (bf16[16,4,4096]{2,1,0:T(4,128)(2,1)S(1)}, bf16[16,4,4096]{2,1,0:T(4,128)(2,1)}, u32[]{:S(2)}) copy-start(bf16[16,4,4096]{2,1,0:T(4,128)(2,1)} %param.12) | copy-start | bytes 1572868
  19.6 119.4 %copy-start.5 = (f32[16,4,4,8,4]{3,4,1,2,0:T(4,128)S(1)}, f32[16,4,4,8,4]{3,4,1,2,0:T(4,128)}, u32[]{:S(2)}) copy-start(f32[16,4,4,8,4]{3,4,1,2,0:T(4,128)} %copy-done.4) | copy-start | bytes 98308
  19.6 119.4 %copy-start.10 = (f32[16,4,4,8,128]{4,3,1,2,0:T(8,128)S(1)}, f32[16,4,4,8,128]{4,3,1,2,0:T(8,128)}, u32[]{:S(2)}) copy-start(f32[16,4,4,8,128]{4,3,1,2,0:T(8,128)} %fusion.4) | copy-start | bytes 3145732
  139.5 1.0 copy-start.8
  139.6 1.7 %copy-start.2 = (f32[512,512]{1,0:T(8,128)S(1)}, f32[512,512]{1,0:T(8,128)}, u32[]{:S(2)}) copy-start(f32[512,512]{1,0:T(8,128)} %get-tuple-element.17) | copy-start | bytes 3145732

commit v2 on v1

--- a/solution.py
+++ b/solution.py
@@ -102,9 +102,7 @@
             x_hbm.at[:, pl.ds(start, LANES)], xbuf.at[slot], x_sem.at[slot]
         )
 
-    order = [(h, q) for h in range(halves) for q in (3, 1)]
-    order += [(h, q) for h in range(halves) for q in (2, 0)]
-    for h, q in order:
+    for h, q in [(h, q) for h in range(halves) for q in (3, 2, 1, 0)]:
         for p in range(q * quarter, (q + 1) * quarter):
             x_copy(h, p).start()
 
@@ -165,6 +163,8 @@
             for d in range(1, T):
                 forward(d).start()
 
+    chunks = [(c, h) for c in range(parts) for h in range(halves)]
+
     def multiply(h, q, store):
         for p in range(q * quarter, (q + 1) * quarter):
             x_copy(h, p).wait()
@@ -208,41 +208,59 @@
             dst_ref=k_r[stage - 1].at[k],
             send_sem=k_ssem.at[stage - 1, k],
             recv_sem=k_rsem.at[stage - 1, k],
-            device_id=partner(stage),
+            device_id=partner(plan(c, h)[stage - 1][0]),
             device_id_type=MESH,
         )
 
+    def plan(c, h):
+        bits = list(range(1, stages))
+        if c == 0 and h == 0 and len(chunks) > 1:
+            bits = bits[1:] + bits[:1]
+        kept = list(range(n // 2))
+        steps = []
+        for bit in bits:
+            mask = n >> (bit + 1)
+            steps.append((bit, [p for p in kept if p & mask], [p for p in kept if not p & mask]))
+            kept = steps[-1][2]
+        return steps
+
+    arrived = set()
+
+    def paired(p, c, h):
+        q = p // quarter
+        if (h, q) not in arrived:
+            a_copy(h, q).wait_recv()
+            arrived.add((h, q))
+        cs = pl.ds(c * CHUNK, CHUNK)
+        return acc[h, p, cs, :] + a_recv[h, q, p % quarter, cs, :].astype(F32)
+
     def first_send(c, h):
-        cs = pl.ds(c * CHUNK, CHUNK)
-        for i in range(quarter):
-            k_s[0][c * halves + h, i] = (
-                acc[h, quarter + i, cs, :] + a_recv[h, 1, i, cs, :].astype(F32)
-            ).astype(BF16)
+        for i, p in enumerate(plan(c, h)[0][1]):
+            k_s[0][c * halves + h, i] = paired(p, c, h).astype(BF16)
         k_copy(1, c, h).start()
 
     def reduce(stage, c, h):
         cs = pl.ds(c * CHUNK, CHUNK)
         k = c * halves + h
-        count = n >> (stage + 1)
+        steps = plan(c, h)
+        kept = steps[stage - 1][2]
+        last = stage == stages - 1
+        going = [] if last else steps[stage][1]
         k_copy(stage, c, h).wait_recv()
-        if stage == 1 and c == 0:
-            a_copy(h, 0).wait_recv()
-        last = stage == stages - 1
-        for i in range(count - 1, -1, -1):
-            value = acc[h, i, cs, :] + k_r[stage - 1][k, i].astype(F32)
-            if stage == 1:
-                value = value + a_recv[h, 0, i, cs, :].astype(F32)
+        for p in going + [p for p in kept if p not in going]:
+            value = paired(p, c, h) if stage == 1 else acc[h, p, cs, :]
+            value = value + k_r[stage - 1][k, kept.index(p)].astype(F32)
             if last:
                 value = value.T
                 hs = pl.ds(h * LANES, LANES)
                 grad[hs, cs] = value
                 u[hs, cs] = (w[hs, cs].astype(F32) - step_size * value).astype(BF16)
-            elif i >= count // 2:
-                k_s[stage][k, i - count // 2] = value.astype(BF16)
+            elif p in going:
+                k_s[stage][k, going.index(p)] = value.astype(BF16)
+                if p == going[-1]:
+                    k_copy(stage + 1, c, h).start()
             else:
-                acc[h, i, cs, :] = value
-            if not last and i == count // 2:
-                k_copy(stage + 1, c, h).start()
+                acc[h, p, cs, :] = value
 
     def n_copy(stage, c):
         return pltpu.make_async_remote_copy(
@@ -285,23 +303,25 @@
             n_copy(stage + 1, c).start()
             nva[c, : count // 2] = value[: count // 2]
 
-    chunks = [(c, h) for c in range(parts) for h in range(halves)]
-
-    for_partner(0, 1)
-    for_self(0, 1)
-    for h in range(1, halves):
+    sent = set()
+
+    def send_chunk(j):
+        if j < len(chunks) and j not in sent:
+            sent.add(j)
+            first_send(*chunks[j])
+
+    for h in range(halves):
         for_partner(h, 1)
-    a_copy(0, 1).wait_recv()
-    first_send(0, 0)
-    for h in range(1, halves):
+        for_partner(h, 0)
         for_self(h, 1)
-        a_copy(h, 1).wait_recv()
-    for c, h in chunks[1:]:
-        first_send(c, h)
-    for h in range(halves):
-        for_partner(h, 0)
-    for h in range(halves):
+        if h == 0:
+            send_chunk(halves)
+        else:
+            send_chunk(h)
         for_self(h, 0)
+        if h == 0:
+            send_chunk(0)
+    send_chunk(1)
     pass_on()
 
     pending = []
@@ -328,6 +348,7 @@
 
     for j in range(len(chunks) + stages):
         stage_of(1, j)
+        send_chunk(j + 3)
         for stage in range(3, stages):
             stage_of(stage, j - (stage - 2))
         slot()

time: 142 us -> 127 us (0.89)
  Pallas kernels: 119 us -> 103 us
    pallas_call x1, Pallas kernels: 119 us -> 103 us  [exchange(): pl.pallas_call(functools.partial(kernel, F, T, stages), out_shape=(jax.Sh...]
where the time goes in v2:
time: 127 us
  Pallas kernels  103 us (81%)
  local copies, waits for them, and re-layouts  12.7 us (10%)
  matrix products  8.75 us (7%)
  other arithmetic  1.42 us (1%)
    pallas_call x1, Pallas kernels, exchange(): pl.pallas_call(functools.partial(kernel, F, T, stages), out_shape=(jax.Sh...  103 us
    dot_general x1, matrix products, attend_rows(): jnp.einsum('rsgqp,rpgd->rsgqd', cache_weights, cached_values, preferred_e...  3.39 us
    unnamed x26, local copies, waits for them, and re-layouts  3.22 us
    reshape x1, local copies, waits for them, and re-layouts, attend_rows(): cached_keys = cache_keys.reshape(row_count, slot_count, group_count, HD)  2.56 us

profile of v2, /device:TPU:0, one launch (start us, length us, event | category | flops | bytes accessed | tf_op | source)
XLA Modules:
  0.0 126.9 jit_solution(8702844522120702417)
XLA Ops:
  0.6 0.0 copy-start
  0.6 2.4 %reshape.69 = bf16[16,4,4,8,128]{4,3,2,1,0:T(8,128)(2,1)} reshape(bf16[16,4,4096]{2,1,0:T(4,128)(2,1)} %param.13) | data formatting | bytes 1048576 | tf_op jit(solution)/shard_map/reshape | solution.py:29
  3.1 2.6 %reshape.68 = bf16[16,128,4,128]{3,2,1,0:T(4,128)(2,1)S(1)} reshape(bf16[16,128,512]{2,1,0:T(8,128)(2,1)} %param.15) | data formatting | bytes 4194304 | tf_op jit(solution)/shard_map/reshape | solution.py:30
  5.6 0.0 copy-done.9
  5.6 0.1 iota_compare_fusion
  5.7 2.4 %fusion.30 = (f32[16,4,4,8]{3,1,2,0:T(4,128)S(1)}, f32[16,4,4,8,128]{4,3,1,2,0:T(8,128)S(1)}) fusion(bf16[16,4,4,8,128]{4,3,2,1,0:T(8,128)(2,1)} %reshape.69, bf16[16,128,4,128,1]{3,2,1,0,4:T(4,128)(2,1)S(1)} %bitcast.29, pred[16,128]{1,0:T(8,128)(4,1)S(1)} %iota_compare_fusion), kind=kOutput, calls=%fused_computation.30 | convolution fusion | flops 67893248 | bytes 3680256 | tf_op jit(solution)/shard_map/rsgqd,rpgd->rsgqp/dot_general | solution.py:35
  8.1 0.0 copy-done
  8.2 0.0 copy-done.7
  8.2 0.0 copy-start.1
  8.2 2.5 %fusion.31 = (f32[16,4,4,8]{3,1,2,0:T(4,128)S(1)}, f32[16,4,4,8,4]{3,4,1,2,0:T(4,128)S(1)}) fusion(bf16[16,4,4,8,128]{4,3,2,1,0:T(8,128)(2,1)S(1)} %copy-done.7, bf16[16,4,512]{2,1,0:T(4,128)(2,1)S(1)} %copy-done, pred[4,4]{1,0:T(4,128)(4,1)S(1)} %iota_compare_fusion.1), kind=kOutput, calls=%fused_computation.31 | convolution fusion | flops 2119680 | bytes 630800 | tf_op jit(solution)/shard_map/rsgqd,rugd->rsgqu/dot_general | solution.py:41
  10.6 0.0 copy-start.4
  10.6 0.1 max.7
  10.7 0.8 fusion.20
  11.5 0.0 copy-done.4
  11.5 0.5 fusion.25
  12.0 0.0 copy-done.1
  12.0 2.1 %reshape.71 = bf16[16,128,4,128]{3,2,1,0:T(4,128)(2,1)} reshape(bf16[16,128,512]{2,1,0:T(8,128)(2,1)S(1)} %copy-done.1) | data formatting | bytes 4194304 | tf_op jit(solution)/shard_map/reshape | solution.py:31
  14.1 3.4 %fusion.4 = f32[16,4,4,8,128]{4,3,1,2,0:T(8,128)} fusion(bf16[16,128,4,128,1]{3,2,1,0,4:T(4,128)(2,1)} %bitcast.30, f32[16,4,4,8,128]{4,3,1,2,0:T(8,128)S(1)} %get-tuple-element.11, f32[16,4,4,8]{3,1,2,0:T(4,128)S(1)} %add.10, f32[16,4,4,8]{3,1,2,0:T(4,128)S(1)} %max.7), kind=kOutput, calls=%fused_computation.4 | convolution fusion | flops 67895296 | bytes 4210688 | tf_op jit(solution)/shard_map/rsgqp,rpgd->rsgqd/dot_general | solution.py:55
  17.5 1.2 copy.19
  18.7 0.9 reshape.66.dec
  19.6 103.2 %shard_map.112 = (f32[512,512]{1,0:T(8,128)}, bf16[64,512]{1,0:T(8,128)(2,1)}) custom-call(bf16[768,8192]{1,0:T(8,128)(2,1)} %x_hbm.1, bf16[512,768]{1,0:T(8,128)(2,1)} %bitcast.31, bf16[512,512]{1,0:T(8,128)(2,1)} %w.1, bf16[64,4096]{1,0:T(8,128)(2,1)} %reshape.66.dec), custom_call_target="tpu_custom_call" | custom-call | flops 6442450944 | bytes 12582912 | tf_op jit(solution)/shard_map/pallas_call | solution.py:398
  122.8 0.9 reshape_reshape.3
  123.7 0.0 copy-done.5
  123.7 0.0 copy-done.10
  123.7 0.5 fusion.17
  124.2 0.0 copy-start.8
  124.2 0.0 copy-start.2
  124.2 0.1 copy.38
  124.3 0.9 reshape.77
  125.2 0.6 reshape.67
  125.9 0.0 copy-done.2
  125.9 1.0 copy.65
  (11 shorter events, 0.1 us)
Async XLA Ops:
  0.6 7.5 %copy-start = (bf16[16,4,512]{2,1,0:T(4,128)(2,1)S(1)}, bf16[16,4,512]{2,1,0:T(4,128)(2,1)}, u32[]{:S(2)}) copy-start(bf16[16,4,512]{2,1,0:T(4,128)(2,1)} %param.14) | copy-start | bytes 196612
  3.1 2.6 %copy-start.9 = (s32[16]{0:T(128)S(1)}, s32[16]{0:T(128)}, u32[]{:S(2)}) copy-start(s32[16]{0:T(128)} %param.17) | copy-start | bytes 196
  5.7 2.4 %copy-start.7 = (bf16[16,4,4,8,128]{4,3,2,1,0:T(8,128)(2,1)S(1)}, bf16[16,4,4,8,128]{4,3,2,1,0:T(8,128)(2,1)}, u32[]{:S(2)}) copy-start(bf16[16,4,4,8,128]{4,3,2,1,0:T(8,128)(2,1)} %reshape.69) | copy-start | bytes 1572868
  8.2 3.8 %copy-start.1 = (bf16[16,128,512]{2,1,0:T(8,128)(2,1)S(1)}, bf16[16,128,512]{2,1,0:T(8,128)(2,1)}, u32[]{:S(2)}) copy-start(bf16[16,128,512]{2,1,0:T(8,128)(2,1)} %param.16) | copy-start | bytes 6291460
  10.6 0.8 copy-start.4
  14.1 3.4 %copy-start.3 = (bf16[768,512]{1,0:T(8,128)(2,1)S(1)}, bf16[768,512]{1,0:T(8,128)(2,1)}, u32[]{:S(2)}) copy-start(bf16[768,512]{1,0:T(8,128)(2,1)} %param.10) | copy-start | bytes 2359300
  14.1 4.6 %copy-start.6 = (bf16[16,4,4096]{2,1,0:T(4,128)(2,1)S(1)}, bf16[16,4,4096]{2,1,0:T(4,128)(2,1)}, u32[]{:S(2)}) copy-start(bf16[16,4,4096]{2,1,0:T(4,128)(2,1)} %param.12) | copy-start | bytes 1572868
  19.6 104.1 %copy-start.5 = (f32[16,4,4,8,4]{3,4,1,2,0:T(4,128)S(1)}, f32[16,4,4,8,4]{3,4,1,2,0:T(4,128)}, u32[]{:S(2)}) copy-start(f32[16,4,4,8,4]{3,4,1,2,0:T(4,128)} %copy-done.4) | copy-start | bytes 98308
  19.6 104.1 %copy-start.10 = (f32[16,4,4,8,128]{4,3,1,2,0:T(8,128)S(1)}, f32[16,4,4,8,128]{4,3,1,2,0:T(8,128)}, u32[]{:S(2)}) copy-start(f32[16,4,4,8,128]{4,3,1,2,0:T(8,128)} %fusion.4) | copy-start | bytes 3145732
  124.2 1.0 copy-start.8
  124.2 1.7 %copy-start.2 = (f32[512,512]{1,0:T(8,128)S(1)}, f32[512,512]{1,0:T(8,128)}, u32[]{:S(2)}) copy-start(f32[512,512]{1,0:T(8,128)} %get-tuple-element.17) | copy-start | bytes 3145732

commit v3 on v2

--- a/solution.py
+++ b/solution.py
@@ -19,51 +19,9 @@
 F32 = jnp.float32
 
 
-def attend_rows(queries, new_keys, new_values, cache_keys, cache_values, lengths):
-    row_count = queries.shape[0]
-    step_count = queries.shape[1]
-    slot_count = cache_keys.shape[1]
-    group_count = cache_keys.shape[2] // HD
-    per_group = QH // KVH
-    factor = 1.0 / math.sqrt(HD)
-    query_heads = queries.reshape(row_count, step_count, group_count, per_group, HD)
-    cached_keys = cache_keys.reshape(row_count, slot_count, group_count, HD)
-    cached_values = cache_values.reshape(row_count, slot_count, group_count, HD)
-    fresh_keys = new_keys.reshape(row_count, step_count, group_count, HD)
-    fresh_values = new_values.reshape(row_count, step_count, group_count, HD)
-    cache_scores = (
-        jnp.einsum("rsgqd,rpgd->rsgqp", query_heads, cached_keys, preferred_element_type=F32)
-        * factor
-    )
-    live_slots = jnp.arange(slot_count, dtype=jnp.int32)[None, :] < lengths[:, None]
-    cache_scores = jnp.where(live_slots[:, None, None, None, :], cache_scores, -1e30)
-    fresh_scores = (
-        jnp.einsum("rsgqd,rugd->rsgqu", query_heads, fresh_keys, preferred_element_type=F32)
-        * factor
-    )
-    causal = (
-        jnp.arange(step_count, dtype=jnp.int32)[None, :]
-        <= jnp.arange(step_count, dtype=jnp.int32)[:, None]
-    )
-    fresh_scores = jnp.where(causal[None, :, None, None, :], fresh_scores, -1e30)
-    highest = jnp.maximum(jnp.max(cache_scores, axis=-1), jnp.max(fresh_scores, axis=-1))
-    cache_exp = jnp.exp(cache_scores - highest[..., None])
-    fresh_exp = jnp.exp(fresh_scores - highest[..., None])
-    denominator = jnp.sum(cache_exp, axis=-1) + jnp.sum(fresh_exp, axis=-1)
-    cache_weights = (cache_exp / denominator[..., None]).astype(BF16)
-    fresh_weights = (fresh_exp / denominator[..., None]).astype(BF16)
-    mixed = jnp.einsum(
-        "rsgqp,rpgd->rsgqd", cache_weights, cached_values, preferred_element_type=F32
-    )
-    mixed = mixed + jnp.einsum(
-        "rsgqu,rugd->rsgqd", fresh_weights, fresh_values, preferred_element_type=F32
-    )
-    return mixed.astype(BF16).reshape(row_count, step_count, group_count * per_group * HD)
-
-
 def kernel(
-    F, T, stages, x_hbm, dyt, w, dec, grad, nv,
-    xbuf, acc, a_send, a_recv, decpos, u, nva, *rest
+    F, T, stages, x_hbm, dyt, w, dec, q_ref, nk, ck_hbm, cv_hbm, lengths, grad, nv, out,
+    ck, cv, cache_sem, mixed, fresh, xbuf, acc, a_send, a_recv, decpos, u, nva, *rest
 ):
     n = 2 * F
     k_s = rest[: stages - 1]
@@ -106,6 +64,13 @@
         for p in range(q * quarter, (q + 1) * quarter):
             x_copy(h, p).start()
 
+    cache_copies = [
+        pltpu.make_async_copy(ck_hbm, ck, cache_sem.at[0]),
+        pltpu.make_async_copy(cv_hbm, cv, cache_sem.at[1]),
+    ]
+    for copy in cache_copies:
+        copy.start()
+
     barrier = pltpu.get_barrier_semaphore()
     for p in range(1, n):
         g2, f2 = place(p)
@@ -164,6 +129,43 @@
                 forward(d).start()
 
     chunks = [(c, h) for c in range(parts) for h in range(halves)]
+
+    rows, groups, heads = q_ref.shape[:3]
+    steps_per_row = tokens // rows
+    factor = 1.0 / math.sqrt(HD)
+    by_rows = (((1,), (1,)), ((), ()))
+
+    def attend(r, _):
+        slots = lax.broadcasted_iota(jnp.int32, (heads, ck.shape[1]), 1)
+        live = slots < lengths[r]
+        token = lax.broadcasted_iota(jnp.int32, (heads, tokens), 1) - r * steps_per_row
+        step = lax.broadcasted_iota(jnp.int32, (heads, tokens), 0) >> 3
+        causal = (token >= 0) & (token <= step)
+        for group in range(groups):
+            gs = pl.ds(group * HD, HD)
+            query = q_ref[r, group]
+            old = lax.dot_general(query, ck[r, :, gs], by_rows, preferred_element_type=F32)
+            old = jnp.where(live, old * factor, -1e30)
+            new = lax.dot_general(query, nk[:, gs], by_rows, preferred_element_type=F32)
+            new = jnp.where(causal, new * factor, -1e30)
+            highest = jnp.maximum(
+                jnp.max(old, axis=-1, keepdims=True), jnp.max(new, axis=-1, keepdims=True)
+            )
+            old = jnp.exp(old - highest)
+            new = jnp.exp(new - highest)
+            total = jnp.sum(old, axis=-1, keepdims=True) + jnp.sum(new, axis=-1, keepdims=True)
+            fresh[group, r] = (new / total).astype(BF16)
+            mixed[group, r] = jnp.dot(
+                (old / total).astype(BF16), cv[r, :, gs], preferred_element_type=F32
+            )
+        return 0
+
+    def complete(group):
+        weights = fresh[group].reshape(rows * heads, tokens)
+        added = jnp.dot(
+            weights, nv[:, group * HD : (group + 1) * HD], preferred_element_type=F32
+        )
+        out[group] = (mixed[group] + added.reshape(rows, heads, HD)).astype(BF16)
 
     def multiply(h, q, store):
         for p in range(q * quarter, (q + 1) * quarter):
@@ -298,6 +300,8 @@
         value = nva[c, :count] + n_r[stage][c].astype(F32)
         if stage == stages - 1:
             nv[:, c * CHUNK : (c + 1) * CHUNK] = value[0].astype(BF16)
+            ready.append(c)
+            flush()
         else:
             n_s[stage + 1][c] = value[count // 2 :].astype(BF16)
             n_copy(stage + 1, c).start()
@@ -324,6 +328,20 @@
     send_chunk(1)
     pass_on()
 
+    ready = []
+    attended_rows = [0]
+
+    def flush():
+        while ready and attended_rows[0] == rows:
+            complete(ready.pop(0))
+
+    def attend_some(count):
+        first = attended_rows[0]
+        if first < rows:
+            attended_rows[0] = min(rows, first + count)
+            lax.fori_loop(first, attended_rows[0], attend, 0)
+        flush()
+
     pending = []
 
     def slot():
@@ -346,6 +364,9 @@
             if stage == stages - 1:
                 finish(j)
 
+    for copy in cache_copies:
+        copy.wait()
+    portion = -(-rows // max(1, parts * halves - 3))
     for j in range(len(chunks) + stages):
         stage_of(1, j)
         send_chunk(j + 3)
@@ -354,8 +375,10 @@
         slot()
         if j < len(chunks) - 1:
             slot()
+        attend_some(portion)
         stage_of(2, j)
         slot()
+    attend_some(rows)
     while pending:
         slot()
 
@@ -378,7 +401,7 @@
             forward(d).wait_send()
 
 
-def exchange(F, T, x, dyt, w, dec):
+def exchange(F, T, x, dyt, w, dec, q, nk, ck, cv, lengths):
     n = 2 * F
     stages = n.bit_length() - 1
     cols = dyt.shape[0]
@@ -388,6 +411,7 @@
     parts = cols // CHUNK
     tokens = dec.shape[0]
     count = halves * parts
+    rows, groups, heads = q.shape[:3]
     dma = pltpu.SemaphoreType.DMA
     k_bufs = [
         pltpu.VMEM((count, n >> (s + 1), CHUNK, LANES), BF16) for s in range(1, stages)
@@ -400,10 +424,19 @@
         out_shape=(
             jax.ShapeDtypeStruct((block, cols), F32),
             jax.ShapeDtypeStruct((tokens, cols), BF16),
+            jax.ShapeDtypeStruct((groups, rows, heads, HD), BF16),
         ),
-        in_specs=[hbm, vmem, vmem, hbm],
-        out_specs=(vmem, vmem),
+        in_specs=[
+            hbm, vmem, vmem, hbm, vmem, vmem, hbm, hbm,
+            pl.BlockSpec(memory_space=pltpu.SMEM),
+        ],
+        out_specs=(vmem, vmem, vmem),
         scratch_shapes=[
+            pltpu.VMEM(ck.shape, BF16),
+            pltpu.VMEM(cv.shape, BF16),
+            dma((2,)),
+            pltpu.VMEM((groups, rows, heads, HD), F32),
+            pltpu.VMEM((groups, rows, heads, tokens), BF16),
             pltpu.VMEM((halves * n, held, LANES), BF16),
             pltpu.VMEM((halves, n // 2, cols, LANES), F32),
             pltpu.VMEM((halves, 2, n // 4, cols, LANES), BF16),
@@ -434,7 +467,7 @@
         cost_estimate=pl.CostEstimate(
             flops=2 * held * D * cols, bytes_accessed=held * D * 2, transcendentals=0
         ),
-    )(x, dyt, w, dec)
+    )(x, dyt, w, dec, q, nk, ck, cv, lengths)
 
 
 def shards(
@@ -451,16 +484,28 @@
     lengths,
 ):
     rows, steps, features = decode_inputs.shape
-    gradient, flat_values = exchange(
+    groups = new_keys.shape[2] // HD
+    per_group = QH // KVH
+    by_group = queries.reshape(rows, steps, groups, per_group, HD).transpose(0, 2, 1, 3, 4)
+    gradient, flat_values, mixed = exchange(
         F,
         T,
         normed_inputs,
         value_cotangent.T,
         value_weight,
         decode_inputs.reshape(rows * steps, features),
+        by_group.reshape(rows, groups, steps * per_group, HD),
+        new_keys.reshape(rows * steps, groups * HD),
+        cache_keys,
+        cache_values,
+        lengths,
     )
     new_values = flat_values.reshape(rows, steps, flat_values.shape[1])
-    attended = attend_rows(queries, new_keys, new_values, cache_keys, cache_values, lengths)
+    attended = (
+        mixed.reshape(groups, rows, steps, per_group, HD)
+        .transpose(1, 2, 0, 3, 4)
+        .reshape(rows, steps, groups * per_group * HD)
+    )
     return (gradient, new_values, attended)
 
 

time: 127 us -> 129 us (1.016)
  Pallas kernels: 103 us -> 116 us
  matrix products: 8.75 us -> 0 us
  other arithmetic: 1.42 us -> 0 us
    pallas_call x1, Pallas kernels: 103 us -> 116 us  [exchange(): pl.pallas_call(functools.partial(kernel, F, T, stages), out_shape=(jax.Sh...]
    dot_general x4 -> x0, matrix products: 8.75 us -> none  [the longest x1 3.39 us: attend_rows(): jnp.einsum('rsgqp,rpgd->rsgqd', cache_weights, cached_values, preferred_e...]
    reshape x3 -> x4, local copies, waits for them, and re-layouts: 7.05 us -> 4.96 us  [the longest x2 2.48 us: shards(): queries.reshape(rows, steps, groups, per_group, HD).transpose(0, 2, 1, 3, 4)]
    unnamed x26 -> x6, local copies, waits for them, and re-layouts: 3.22 us -> 2.13 us
where the time goes in v3:
time: 129 us; the launch traced here: 128 us
  Pallas kernels  116 us (90%)
  local copies, waits for them, and re-layouts  11.8 us (9%)
    pallas_call x1, Pallas kernels, exchange(): pl.pallas_call(functools.partial(kernel, F, T, stages), out_shape=(jax.Sh...  116 us

profile of v3, /device:TPU:0, one launch (start us, length us, event | category | flops | bytes accessed | tf_op | source)
XLA Modules:
  0.0 128.2 jit_solution(3374340947475230781)
XLA Ops:
  0.6 0.0 copy-start.1
  0.6 1.6 %reshape.30.nk = bf16[64,512]{1,0:T(8,128)(2,1)} reshape(bf16[16,4,512]{2,1,0:T(4,128)(2,1)} %param.14) | data formatting | bytes 131072 | tf_op jit(solution)/shard_map/reshape | solution.py:498
  2.2 2.0 %reshape.27.dec = bf16[64,4096]{1,0:T(8,128)(2,1)} reshape(bf16[16,4,4096]{2,1,0:T(4,128)(2,1)} %param.12) | data formatting | bytes 1048576 | tf_op jit(solution)/shard_map/reshape | solution.py:496
  4.2 1.6 %reshape.28 = bf16[16,4,4,8,128]{4,3,2,1,0:T(8,128)(2,1)S(1)} reshape(bf16[16,4,4096]{2,1,0:T(4,128)(2,1)} %param.13) | data formatting | bytes 1048576 | tf_op jit(solution)/shard_map/reshape | solution.py:489
  5.7 0.9 copy.16
  6.6 0.0 copy-done.1
  6.6 1.2 copy.12
  7.8 115.7 %shard_map.112 = (f32[512,512]{1,0:T(8,128)}, bf16[64,512]{1,0:T(8,128)(2,1)}, bf16[4,16,32,128]{3,2,1,0:T(8,128)(2,1)}) custom-call(bf16[768,8192]{1,0:T(8,128)(2,1)} %x_hbm.1, bf16[512,768]{1,0:T(8,128)(2,1)} %bitcast.11, bf16[512,512]{1,0:T(8,128)(2,1)} %w.1, bf16[64,4096]{1,0:T(8,128)(2,1)} %reshape.27.dec, bf16[16,4,32,128]{3,2,1,0:T(8,128)(2,1)} %bitcast.13, ...), custom_call_target="tpu_custom_call" | custom-call | flops 6442450944 | bytes 12582912 | tf_op jit(solution)/shard_map/pallas_call | solution.py:422
  123.5 0.0 copy-start
  123.5 1.6 %reshape.31 = bf16[16,4,512]{2,1,0:T(4,128)(2,1)} reshape(bf16[64,512]{1,0:T(8,128)(2,1)} %get-tuple-element.7) | data formatting | bytes 131072 | tf_op jit(solution)/shard_map/reshape | solution.py:503
  125.1 1.2 copy.14
  126.3 0.9 reshape.33
  127.2 0.0 copy-done
  127.2 1.0 copy.18
Async XLA Ops:
  0.6 6.0 %copy-start.1 = (bf16[768,512]{1,0:T(8,128)(2,1)S(1)}, bf16[768,512]{1,0:T(8,128)(2,1)}, u32[]{:S(2)}) copy-start(bf16[768,512]{1,0:T(8,128)(2,1)} %param.10) | copy-start | bytes 2359300
  123.5 3.7 %copy-start = (f32[512,512]{1,0:T(8,128)S(1)}, f32[512,512]{1,0:T(8,128)}, u32[]{:S(2)}) copy-start(f32[512,512]{1,0:T(8,128)} %get-tuple-element.12) | copy-start | bytes 3145732

commit v4 on v3

--- a/solution.py
+++ b/solution.py
@@ -320,6 +320,7 @@
         for_self(h, 1)
         if h == 0:
             send_chunk(halves)
+            send_chunk(2 * halves)
         else:
             send_chunk(h)
         for_self(h, 0)
@@ -366,18 +367,15 @@
 
     for copy in cache_copies:
         copy.wait()
-    portion = -(-rows // max(1, parts * halves - 3))
+    portion = -(-rows // max(1, parts * halves - 2))
     for j in range(len(chunks) + stages):
         stage_of(1, j)
         send_chunk(j + 3)
-        for stage in range(3, stages):
-            stage_of(stage, j - (stage - 2))
-        slot()
-        if j < len(chunks) - 1:
+        if j < len(chunks):
+            attend_some(portion)
+        for stage in range(2, stages):
+            stage_of(stage, j - (stage - 1))
             slot()
-        attend_some(portion)
-        stage_of(2, j)
-        slot()
     attend_some(rows)
     while pending:
         slot()

time: 129 us -> 118 us (0.915)
  Pallas kernels: 116 us -> 106 us
    pallas_call x1, Pallas kernels: 116 us -> 106 us  [exchange(): pl.pallas_call(functools.partial(kernel, F, T, stages), out_shape=(jax.Sh...]
where the time goes in v4:
time: 118 us
  Pallas kernels  106 us (90%)
  local copies, waits for them, and re-layouts  11.8 us (10%)
    pallas_call x1, Pallas kernels, exchange(): pl.pallas_call(functools.partial(kernel, F, T, stages), out_shape=(jax.Sh...  106 us
    reshape x2, local copies, waits for them, and re-layouts, shards(): queries.reshape(rows, steps, groups, per_group, HD).transpose(0, 2, 1, 3, 4)  2.48 us

profile of v4, /device:TPU:0, one launch (start us, length us, event | category | flops | bytes accessed | tf_op | source)
XLA Modules:
  0.0 118.2 jit_solution(16223491005480624735)
XLA Ops:
  0.6 0.0 copy-start.1
  0.6 1.6 %reshape.30.nk = bf16[64,512]{1,0:T(8,128)(2,1)} reshape(bf16[16,4,512]{2,1,0:T(4,128)(2,1)} %param.14) | data formatting | bytes 131072 | tf_op jit(solution)/shard_map/reshape | solution.py:496
  2.2 2.0 %reshape.27.dec = bf16[64,4096]{1,0:T(8,128)(2,1)} reshape(bf16[16,4,4096]{2,1,0:T(4,128)(2,1)} %param.12) | data formatting | bytes 1048576 | tf_op jit(solution)/shard_map/reshape | solution.py:494
  4.2 1.6 %reshape.28 = bf16[16,4,4,8,128]{4,3,2,1,0:T(8,128)(2,1)S(1)} reshape(bf16[16,4,4096]{2,1,0:T(4,128)(2,1)} %param.13) | data formatting | bytes 1048576 | tf_op jit(solution)/shard_map/reshape | solution.py:487
  5.7 0.9 copy.16
  6.6 0.0 copy-done.1
  6.6 1.2 copy.12
  7.8 105.7 %shard_map.112 = (f32[512,512]{1,0:T(8,128)}, bf16[64,512]{1,0:T(8,128)(2,1)}, bf16[4,16,32,128]{3,2,1,0:T(8,128)(2,1)}) custom-call(bf16[768,8192]{1,0:T(8,128)(2,1)} %x_hbm.1, bf16[512,768]{1,0:T(8,128)(2,1)} %bitcast.11, bf16[512,512]{1,0:T(8,128)(2,1)} %w.1, bf16[64,4096]{1,0:T(8,128)(2,1)} %reshape.27.dec, bf16[16,4,32,128]{3,2,1,0:T(8,128)(2,1)} %bitcast.13, ...), custom_call_target="tpu_custom_call" | custom-call | flops 6442450944 | bytes 12582912 | tf_op jit(solution)/shard_map/pallas_call | solution.py:420
  113.5 0.0 copy-start
  113.5 1.6 %reshape.31 = bf16[16,4,512]{2,1,0:T(4,128)(2,1)} reshape(bf16[64,512]{1,0:T(8,128)(2,1)} %get-tuple-element.7) | data formatting | bytes 131072 | tf_op jit(solution)/shard_map/reshape | solution.py:501
  115.1 1.2 copy.14
  116.3 0.9 reshape.33
  117.2 0.0 copy-done
  117.2 1.0 copy.18
Async XLA Ops:
  0.6 6.0 %copy-start.1 = (bf16[768,512]{1,0:T(8,128)(2,1)S(1)}, bf16[768,512]{1,0:T(8,128)(2,1)}, u32[]{:S(2)}) copy-start(bf16[768,512]{1,0:T(8,128)(2,1)} %param.10) | copy-start | bytes 2359300
  113.5 3.7 %copy-start = (f32[512,512]{1,0:T(8,128)S(1)}, f32[512,512]{1,0:T(8,128)}, u32[]{:S(2)}) copy-start(f32[512,512]{1,0:T(8,128)} %get-tuple-element.12) | copy-start | bytes 3145732
